TPU v7x, 32 devices: a whole 2x2x4 slice. The times are simulated.
32 devices in a mesh: groups: 2 (over y), sect: 4 (over x, core), tp: 4 (over z).
Axes of the slice: x: 2, y: 2, z: 4, core: 2. Of those that a mesh axis runs over, the one named last changes fastest.
Arguments:
- tokens: bfloat16 [2, 32, 8192], P(None, 'groups', 'tp'), parts along dimension 1, may hold values from -8 to 8, as said below
- gain: bfloat16 [8192], P('tp'), may hold values from 0.25 to 1.75
- w_query: bfloat16 [8192, 8192], P('tp', 'sect'), may hold values from -0.0625 to 0.0625
- w_kv: bfloat16 [8192, 2048], P('tp', 'sect'), may hold values from -0.0625 to 0.0625
- w_out: bfloat16 [8192, 8192], P('sect', 'tp'), may hold values from -0.0625 to 0.0625
- cache: bfloat16 [8, 12288, 2048], P(('groups', 'sect'), 'tp'), parts along dimension 0, may hold values from -122 to 122
- lengths: int32 [8, 4], P(('groups', 'sect')), parts along dimension 0, may hold values from 1 to 8192, as said below
- perm: int32 [32], P('groups'), parts along dimension 0, may hold values from 0 to 15, each once
Outputs:
- mixed: bfloat16 [2, 32, 8192], P(None, 'groups', 'tp'), parts along dimension 1
There are 2 independent parts, one for each index of `groups`. A program takes and returns all parts, laid end to end along the dimension named above; an argument that names none is the same for every part. Nothing has to cross between parts.
Inputs may be any that keep to these rules, and one draw needn't show every extreme that they name: `tokens`: scales vary over the features; features may share an offset across requests and steps. `lengths`: each row sums to 12288; its largest entry is exactly 8192. `perm`: every slot once.
All inputs are finite; a program needn't handle non-finite values.
Results may differ from a plain program's by a relative error of at most 0.0036.
Values may be sent and summed in bfloat16 or wider, within the bound.
A program may use at most 128 MiB of HBM per device.

v0:
```python
import math

import jax
import jax.numpy as jnp
from jax import lax
from jax.sharding import PartitionSpec as P

D = 8192
HEADS = 64
KV_HEADS = 8
HEAD_DIM = 128
STEPS = 2


def rotate(values, places):
    half_dim = values.shape[-1] // 2
    freq_index = jnp.arange(half_dim, dtype=jnp.float32)
    inverse = jnp.exp(-(2.0 * freq_index / values.shape[-1]) * math.log(500000.0))
    angles = places[..., None] * inverse
    cosine = jnp.cos(angles)
    sine = jnp.sin(angles)
    first = values[..., :half_dim]
    second = values[..., half_dim:]
    return jnp.concatenate(
        [first * cosine - second * sine, second * cosine + first * sine], axis=-1
    )


def per_device(tokens, gain, w_query, w_kv, w_out, cache, lengths, perm):
    tp_id = lax.axis_index("tp")
    requests = perm.shape[0]
    req_dev = lengths.shape[1]
    block = cache.shape[1]
    per_kv = HEADS // KV_HEADS
    scale = 1.0 / math.sqrt(HEAD_DIM)
    slot_ids = jnp.arange(requests, dtype=jnp.int32)
    select = (perm[None, :] == slot_ids[:, None]).astype(jnp.bfloat16)
    own_lengths = lengths[0]
    ends = jnp.cumsum(own_lengths)
    places = tp_id * block + jnp.arange(block, dtype=jnp.int32)
    segment = jnp.sum((places[:, None] >= ends[None, :]).astype(jnp.int32), axis=1)
    valid = (segment[None, :] == jnp.arange(req_dev, dtype=jnp.int32)[:, None])[:, None, None, :]
    stored = cache[0].reshape(block, KV_HEADS, 2, HEAD_DIM)
    key_rows = stored[:, :, 0]
    value_rows = stored[:, :, 1]
    earlier_keys = []
    earlier_values = []
    results = []
    for step_index in range(STEPS):
        hidden = tokens[step_index].astype(jnp.float32)
        square_sum = lax.psum(jnp.sum(hidden * hidden, axis=1), "tp")
        inv_rms = lax.rsqrt(square_sum / D + 1e-05)
        normed = (hidden * inv_rms[:, None] * gain.astype(jnp.float32)).astype(jnp.bfloat16)
        part_query = jnp.dot(normed, w_query, preferred_element_type=jnp.float32)
        part_pair = jnp.dot(normed, w_kv, preferred_element_type=jnp.float32)
        summed_query, summed_pair = lax.psum((part_query, part_pair), "tp")
        query = summed_query.astype(jnp.bfloat16)
        key_value = summed_pair.astype(jnp.bfloat16)
        query_slot = jnp.dot(select, query, preferred_element_type=jnp.float32).astype(jnp.bfloat16)
        pair_slot = jnp.dot(select, key_value, preferred_element_type=jnp.float32).astype(
            jnp.bfloat16
        )
        own_query, own_pair = (
            lax.all_to_all(query_slot, "sect", split_axis=0, concat_axis=1, tiled=True),
            lax.all_to_all(pair_slot, "sect", split_axis=0, concat_axis=1, tiled=True),
        )
        positions = (own_lengths + step_index).astype(jnp.float32)
        query_rot = rotate(
            own_query.astype(jnp.float32).reshape(req_dev, KV_HEADS, per_kv, HEAD_DIM),
            positions[:, None, None],
        ).astype(jnp.bfloat16)
        pair_heads = own_pair.reshape(req_dev, KV_HEADS, 2, HEAD_DIM)
        new_key = rotate(pair_heads[:, :, 0].astype(jnp.float32), positions[:, None]).astype(
            jnp.bfloat16
        )
        earlier_keys.append(new_key)
        earlier_values.append(pair_heads[:, :, 1])
        new_keys = jnp.stack(earlier_keys)
        new_values = jnp.stack(earlier_values)
        scores = (
            jnp.einsum("jghd,pgd->jghp", query_rot, key_rows, preferred_element_type=jnp.float32)
            * scale
        )
        local_top = jnp.max(jnp.where(valid, scores, -1e30), axis=3)
        cache_top = lax.pmax(local_top, "tp")
        new_scores = (
            jnp.einsum("jghd,njgd->njgh", query_rot, new_keys, preferred_element_type=jnp.float32)
            * scale
        )
        highest = jnp.maximum(cache_top, jnp.max(new_scores, axis=0))
        weights = jnp.where(valid, jnp.exp(scores - highest[..., None]), 0.0)
        local_blend = jnp.einsum(
            "jghp,pgd->jghd",
            weights.astype(jnp.bfloat16),
            value_rows,
            preferred_element_type=jnp.float32,
        )
        weight_total, blend = lax.psum((jnp.sum(weights, axis=3), local_blend), "tp")
        new_weights = jnp.exp(new_scores - highest[None])
        weight_total = weight_total + jnp.sum(new_weights, axis=0)
        blend = blend + jnp.einsum(
            "njgh,njgd->jghd",
            new_weights.astype(jnp.bfloat16),
            new_values,
            preferred_element_type=jnp.float32,
        )
        attended = (
            (blend / weight_total[..., None])
            .astype(jnp.bfloat16)
            .reshape(req_dev, HEADS * HEAD_DIM)
        )
        returned = lax.all_to_all(attended, "sect", split_axis=1, concat_axis=0, tiled=True)
        attn_rows = jnp.dot(select.T, returned, preferred_element_type=jnp.float32).astype(
            jnp.bfloat16
        )
        partial_out = jnp.dot(attn_rows, w_out, preferred_element_type=jnp.float32)
        summed_out = lax.psum(partial_out, "sect")
        results.append((hidden + summed_out).astype(jnp.bfloat16))
    return jnp.stack(results)


def solution(mesh):
    return jax.shard_map(
        per_device,
        mesh=mesh,
        in_specs=(
            P(None, "groups", "tp"),
            P("tp"),
            P("tp", "sect"),
            P("tp", "sect"),
            P("sect", "tp"),
            P(("groups", "sect"), "tp", None),
            P(("groups", "sect"), None),
            P("groups"),
        ),
        out_specs=P(None, "groups", "tp"),
        check_vma=False,
    )
```

profile of v0, /device:TPU:1, one launch (start us, length us, event | category | flops | bytes accessed | tf_op | source)
XLA Modules:
  0.0 270.1 jit_solution(17995561042704546458)
XLA Ops:
  6.5 1.2 fusion.31
  7.7 0.7 convert_element_type.163
  8.4 10.7 %all-reduce.2 = (f32[16]{0:T(128)S(1)}, f32[16]{0:T(128)S(1)}) all-reduce(f32[16]{0:T(128)S(1)} %get-tuple-element.6, f32[16]{0:T(128)S(1)} %get-tuple-element.5), channel_id=1, replica_groups=mesh['groups'=2,'sect'=4,'tp'=4] {'tp'}, use_global_device_ids=true, to_apply=%region_13.14 | all-reduce | flops 32 | bytes 256 | tf_op jit(solution)/shard_map/psum | solution.py:51
  19.2 4.8 %fusion.65 = f32[16,2048]{1,0:T(8,128)S(1)} fusion(bf16[2048,2048]{1,0:T(8,128)(2,1)} %param.10, f32[16]{0:T(128)S(1)} %get-tuple-element.57, f32[2048]{0:T(1024)S(1)} %convert_element_type.163, bf16[2,16,2048]{2,1,0:T(8,128)(2,1)} %param.8), kind=kOutput, calls=%fused_computation.108 | convolution fusion | flops 134348800 | bytes 8593472 | tf_op jit(solution)/shard_map/dot_general | solution.py:54
  24.0 1.0 copy-done.1
  24.9 1.2 fusion.69
  26.2 0.4 fusion.63
  26.6 0.4 fusion.67
  27.0 18.9 %all-reduce.12 = (bf16[16,2048]{1,0:T(8,128)(2,1)S(1)}, bf16[16,2048]{1,0:T(8,128)(2,1)S(1)}, bf16[16,512]{1,0:T(8,128)(2,1)S(1)}, bf16[16,512]{1,0:T(8,128)(2,1)S(1)}) all-reduce(f32[16,2048]{1,0:T(8,128)S(1)} %fusion.65, f32[16,2048]{1,0:T(8,128)S(1)} %fusion.69, ...), channel_id=1, replica_groups=mesh['groups'=2,'sect'=4,'tp'=4] {'tp'}, use_global_device_ids=true, to_apply=%region_14.15 | all-reduce | flops 81920 | bytes 491520 | tf_op jit(solution)/shard_map/psum | solution.py:56
  45.9 0.1 convolution_convert_fusion.5
  46.1 0.6 all_to_all.74
  46.7 8.7 %all-to-all-start.1 = ((bf16[4,4,512]{2,1,0:T(4,128)(2,1)}), bf16[4,4,512]{2,1,0:T(4,128)(2,1)S(1)}, u32[]{:S(2)}, u32[]{:S(2)}) async-start(bf16[4,4,512]{2,1,0:T(4,128)(2,1)} %all_to_all.74), calls=%async_computation.1 | async-start | bytes 32768 | tf_op jit(solution)/shard_map/all_to_all | solution.py:65
  55.3 0.1 convolution_convert_fusion.3
  55.5 0.2 reduce-window.8
  55.7 0.1 convert_reduce_fusion
  55.8 0.1 convolution_convert_fusion.1
  56.0 0.1 convolution_convert_fusion.4
  56.1 0.1 multiply_cosine_fusion.1
  56.2 0.7 all_to_all.72
  56.9 16.6 %copy.174 = bf16[1,3072,2048]{1,2,0:T(8,128)(2,1)} copy(bf16[1,3072,2048]{2,1,0:T(8,128)(2,1)} %param.13) | data formatting | bytes 25165824 | tf_op args[5]
  73.5 0.7 all_to_all.81
  74.2 0.6 all_to_all.83
  74.8 3.3 %all-to-all-start.4 = ((bf16[4,4,512]{2,1,0:T(4,128)(2,1)}), bf16[4,4,512]{2,1,0:T(4,128)(2,1)S(1)}, u32[]{:S(2)}, u32[]{:S(2)}) async-start(bf16[4,4,512]{2,1,0:T(4,128)(2,1)} %all_to_all.83), calls=%async_computation.4 | async-start | bytes 32768 | tf_op jit(solution)/shard_map/all_to_all | solution.py:65
  78.2 3.1 %all-to-all-done.4 = bf16[4,4,512]{2,1,0:T(4,128)(2,1)S(1)} async-done(((bf16[4,4,512]{2,1,0:T(4,128)(2,1)}), bf16[4,4,512]{2,1,0:T(4,128)(2,1)S(1)}, u32[]{:S(2)}, u32[]{:S(2)}) %all-to-all-start.4) | async-done | bytes 16416 | tf_op jit(solution)/shard_map/all_to_all | solution.py:65
  81.2 4.0 %all-to-all-start = ((bf16[4,4,2048]{2,1,0:T(4,128)(2,1)}), bf16[4,4,2048]{2,1,0:T(4,128)(2,1)S(1)}, u32[]{:S(2)}, u32[]{:S(2)}) async-start(bf16[4,4,2048]{2,1,0:T(4,128)(2,1)} %all_to_all.72), calls=%async_computation | async-start | bytes 131072 | tf_op jit(solution)/shard_map/all_to_all | solution.py:64
  85.3 0.1 subtract_convert_fusion.3
  85.4 0.1 fusion.61
  85.4 0.1 maximum_bitcast_fusion
  85.6 2.9 %all-to-all-done = bf16[4,4,2048]{2,1,0:T(4,128)(2,1)S(1)} async-done(((bf16[4,4,2048]{2,1,0:T(4,128)(2,1)}), bf16[4,4,2048]{2,1,0:T(4,128)(2,1)S(1)}, u32[]{:S(2)}, u32[]{:S(2)}) %all-to-all-start) | async-done | bytes 65568 | tf_op jit(solution)/shard_map/all_to_all | solution.py:64
  88.5 4.1 %all-to-all-start.3 = ((bf16[4,4,2048]{2,1,0:T(4,128)(2,1)}), bf16[4,4,2048]{2,1,0:T(4,128)(2,1)S(1)}, u32[]{:S(2)}, u32[]{:S(2)}) async-start(bf16[4,4,2048]{2,1,0:T(4,128)(2,1)} %all_to_all.81), calls=%async_computation.3 | async-start | bytes 131072 | tf_op jit(solution)/shard_map/all_to_all | solution.py:64
  92.6 0.1 copy.171
  92.7 0.1 reshape.459
  92.8 0.1 fusion.83
  92.9 0.1 pad_maximum_fusion.1
  93.0 5.6 %select_reduce_fusion.1 = (f32[4,8,8]{2,0,1:T(4,128)S(1)}, f32[4,8,8,3072]{3,2,0,1:T(8,128)}) fusion(pred[4,3072]{1,0:T(4,128)(4,1)S(1)} %iota_compare_fusion, bf16[4,8,8,128]{3,2,0,1:T(8,128)(2,1)S(1)} %pad_maximum_fusion.1, bf16[3072,8,2,128]{0,3,2,1:T(8,128)(2,1)} %bitcast.124), kind=kOutput, calls=%fused_computation.13 | convolution fusion | flops 203685632 | bytes 9516032 | tf_op jit(solution)/shard_map/jghd,pgd->jghp/dot_general | solution.py:81
  98.6 0.1 fusion.44
  98.8 13.2 %pmax.14 = f32[4,8,8]{2,0,1:T(4,128)S(1)} all-reduce(f32[4,8,8]{2,0,1:T(4,128)S(1)} %get-tuple-element.52), channel_id=1, replica_groups=mesh['groups'=2,'sect'=4,'tp'=4] {'tp'}, use_global_device_ids=true, to_apply=%region_6.7 | all-reduce | flops 256 | bytes 2048 | tf_op jit(solution)/shard_map/pmax | solution.py:85
  112.0 0.1 copy.181
  112.1 0.1 reshape.463
  112.2 0.1 fusion.84
  112.4 6.7 %fusion.20 = f32[4,8,8,128]{3,2,0,1:T(8,128)} fusion(bf16[3072,8,2,128]{0,3,2,1:T(8,128)(2,1)} %bitcast.125, f32[4,8,8,3072]{3,2,0,1:T(8,128)} %get-tuple-element.53, f32[4,8,8]{2,0,1:T(4,128)S(1)} %fusion.60, pred[4,3072]{1,0:T(4,128)(4,1)S(1)} %iota_compare_fusion), kind=kOutput, calls=%fused_computation.28 | convolution fusion | flops 203685888 | bytes 9581568 | tf_op jit(solution)/shard_map/jghp,pgd->jghd/dot_general | solution.py:92
  119.1 6.4 %fusion.8 = (f32[4,8,8]{2,0,1:T(4,128)S(1)}, f32[4,8,8]{2,0,1:T(4,128)S(1)}, f32[4,8,8,3072]{3,2,0,1:T(8,128)}) fusion(f32[4,8,8,3072]{3,2,0,1:T(8,128)S(1)} %copy-done.2, f32[4,8,8]{2,0,1:T(4,128)S(1)} %fusion.60, pred[4,3072]{1,0:T(4,128)(4,1)S(1)} %iota_compare_fusion, bf16[3072,8,2,128]{0,3,2,1:T(8,128)(2,1)} %bitcast.126, ...), kind=kOutput, calls=%fused_computation.14 | convolution fusion | flops 206175744 | bytes 12663808 | tf_op jit(solution)/shard_map/jghd,pgd->jghp/dot_general | solution.py:81
  125.4 12.2 %pmax.15 = f32[4,8,8]{2,1,0:T(8,128)S(1)} all-reduce(f32[4,8,8]{2,1,0:T(8,128)S(1)} %copy.184), channel_id=1, replica_groups=mesh['groups'=2,'sect'=4,'tp'=4] {'tp'}, use_global_device_ids=true, to_apply=%region_16.17 | all-reduce | flops 256 | bytes 2048 | tf_op jit(solution)/shard_map/pmax | solution.py:85
  137.7 0.3 fusion.85
  138.0 2.8 %fusion.10 = f32[4,8,8]{2,0,1:T(4,128)S(1)} fusion(f32[4,8,8,3072]{3,2,0,1:T(8,128)} %get-tuple-element.54, f32[4,8,8]{2,0,1:T(4,128)S(1)} %copy.191, pred[4,3072]{1,0:T(4,128)(4,1)S(1)} %iota_compare_fusion), kind=kLoop, calls=%fused_computation.16 | loop fusion | flops 2359040 | bytes 3160064 | tf_op jit(solution)/shard_map/reduce_sum | solution.py:98
  140.8 5.6 %fusion.23 = f32[4,8,8,128]{3,2,0,1:T(8,128)} fusion(bf16[3072,8,2,128]{0,3,2,1:T(8,128)(2,1)} %bitcast.127, f32[4,8,8,3072]{3,2,0,1:T(8,128)S(1)} %copy-done.3, f32[4,8,8]{2,0,1:T(4,128)S(1)} %copy.191, pred[4,3072]{1,0:T(4,128)(4,1)S(1)} %iota_compare_fusion), kind=kOutput, calls=%fused_computation.29 | convolution fusion | flops 203685888 | bytes 9581568 | tf_op jit(solution)/shard_map/jghp,pgd->jghd/dot_general | solution.py:92
  146.4 0.1 fusion.47
  146.5 12.7 %all-reduce = (f32[4,8,8]{2,0,1:T(4,128)S(1)}, f32[4,8,8]{2,0,1:T(4,128)S(1)}) all-reduce(f32[4,8,8]{2,0,1:T(4,128)S(1)} %fusion.10, f32[4,8,8]{2,0,1:T(4,128)S(1)} %get-tuple-element.7), channel_id=1, replica_groups=mesh['groups'=2,'sect'=4,'tp'=4] {'tp'}, use_global_device_ids=true, to_apply=%region_21.22 | all-reduce | flops 512 | bytes 4096 | tf_op jit(solution)/shard_map/psum | solution.py:98
  159.2 0.0 all-reduce.9.cloned.1.call-update
  159.2 43.9 %all-reduce.9.cloned.1.call-done = (f32[4,8,8,128]{3,2,0,1:T(8,128)}, f32[4,8,8,128]{3,2,0,1:T(8,128)}) async-done(((f32[4,8,8,128]{3,2,0,1:T(8,128)}, f32[4,8,8,128]{3,2,0,1:T(8,128)}), (f32[4,8,8,128]{3,2,0,1:T(8,128)}, f32[4,8,8,128]{3,2,0,1:T(8,128)})) %all-reduce.9.cloned.1.call-update) | async-done | bytes 262160 | tf_op jit(solution)/shard_map/psum | solution.py:98
  203.1 1.0 divide_convert_fusion
  204.2 0.7 copy.180
  204.9 5.4 %all-to-all-start.2 = ((bf16[4,4,2048]{2,0,1:T(4,128)(2,1)}), bf16[4,4,2048]{2,0,1:T(4,128)(2,1)S(1)}, u32[]{:S(2)}, u32[]{:S(2)}) async-start(bf16[4,4,2048]{2,0,1:T(4,128)(2,1)} %copy.180), calls=%async_computation.2 | async-start | bytes 131072 | tf_op jit(solution)/shard_map/all_to_all | solution.py:112
  210.3 1.1 fusion.27
  211.5 0.7 copy.197
  212.1 1.4 all-to-all-done.2
  213.5 4.1 %all-to-all-start.5 = ((bf16[4,4,2048]{2,0,1:T(4,128)(2,1)}), bf16[4,4,2048]{2,0,1:T(4,128)(2,1)S(1)}, u32[]{:S(2)}, u32[]{:S(2)}) async-start(bf16[4,4,2048]{2,0,1:T(4,128)(2,1)} %copy.197), calls=%async_computation.5 | async-start | bytes 131072 | tf_op jit(solution)/shard_map/all_to_all | solution.py:112
  217.7 3.2 %all-to-all-done.5 = bf16[4,4,2048]{2,0,1:T(4,128)(2,1)S(1)} async-done(((bf16[4,4,2048]{2,0,1:T(4,128)(2,1)}), bf16[4,4,2048]{2,0,1:T(4,128)(2,1)S(1)}, u32[]{:S(2)}, u32[]{:S(2)}) %all-to-all-start.5) | async-done | bytes 65568 | tf_op jit(solution)/shard_map/all_to_all | solution.py:112
  220.9 5.4 %fusion.28 = f32[16,2048]{1,0:T(8,128)} fusion(bf16[2048,2048]{1,0:T(8,128)(2,1)} %param.12, bf16[16,2048]{1,0:T(8,128)(2,1)S(1)} %all_to_all.80, s32[16]{0:T(128)S(1)} %copy-done.5), kind=kOutput, calls=%fused_computation.33 | convolution fusion | flops 135299328 | bytes 8585280 | tf_op jit(solution)/shard_map/dot_general | solution.py:116
  226.3 5.4 %fusion.29 = f32[16,2048]{1,0:T(8,128)} fusion(bf16[2048,2048]{1,0:T(8,128)(2,1)} %param.12, bf16[16,2048]{1,0:T(8,128)(2,1)S(1)} %all_to_all.89, s32[16]{0:T(128)S(1)} %copy-done.5), kind=kOutput, calls=%fused_computation.34 | convolution fusion | flops 135299328 | bytes 8585280 | tf_op jit(solution)/shard_map/dot_general | solution.py:116
  231.7 0.0 all-reduce.11.cloned.1.call-update
  231.8 29.9 %all-reduce.11.cloned.1.call-done = (f32[16,2048]{1,0:T(8,128)}, f32[16,2048]{1,0:T(8,128)}) async-done(((f32[16,2048]{1,0:T(8,128)}, f32[16,2048]{1,0:T(8,128)}), (f32[16,2048]{1,0:T(8,128)}, f32[16,2048]{1,0:T(8,128)})) %all-reduce.11.cloned.1.call-update) | async-done | bytes 262160 | tf_op jit(solution)/shard_map/psum | solution.py:117
  261.6 1.0 fusion.40
  262.7 0.6 copy-done.6
  (51 shorter events, 0.5 us)
Async XLA Ops:
  6.5 19.6 %copy-start = (bf16[2048,512]{1,0:T(8,128)(2,1)S(1)}, bf16[2048,512]{1,0:T(8,128)(2,1)}, u32[]{:S(2)}) copy-start(bf16[2048,512]{1,0:T(8,128)(2,1)} %param.11) | copy-start | bytes 6291460
  19.1 5.8 %copy-start.1 = (bf16[2048,2048]{1,0:T(8,128)(2,1)S(1)}, bf16[2048,2048]{1,0:T(8,128)(2,1)}, u32[]{:S(2)}) copy-start(bf16[2048,2048]{1,0:T(8,128)(2,1)} %param.10) | copy-start | bytes 25165828
  19.1 5.8 %copy-start.4 = (bf16[2,16,2048]{2,1,0:T(8,128)(2,1)S(1)}, bf16[2,16,2048]{2,1,0:T(8,128)(2,1)}, u32[]{:S(2)}) copy-start(bf16[2,16,2048]{2,1,0:T(8,128)(2,1)} %param.8) | copy-start | bytes 393220
  26.2 19.7 %copy-start.5 = (s32[16]{0:T(128)S(1)}, s32[16]{0:T(128)}, u32[]{:S(2)}) copy-start(s32[16]{0:T(128)} %param.15) | copy-start | bytes 196
  26.2 29.3 %copy-start.7 = (s32[1,4]{1,0:T(1,128)S(1)}, s32[1,4]{1,0:T(1,128)}, u32[]{:S(2)}) copy-start(s32[1,4]{1,0:T(1,128)} %param.14) | copy-start | bytes 52
  46.7 28.1 %all-to-all-start.1 = ((bf16[4,4,512]{2,1,0:T(4,128)(2,1)}), bf16[4,4,512]{2,1,0:T(4,128)(2,1)S(1)}, u32[]{:S(2)}, u32[]{:S(2)}) async-start(bf16[4,4,512]{2,1,0:T(4,128)(2,1)} %all_to_all.74), calls=%async_computation.1 | async-start | bytes 32768 | tf_op jit(solution)/shard_map/all_to_all | solution.py:65
  74.8 6.4 %all-to-all-start.4 = ((bf16[4,4,512]{2,1,0:T(4,128)(2,1)}), bf16[4,4,512]{2,1,0:T(4,128)(2,1)S(1)}, u32[]{:S(2)}, u32[]{:S(2)}) async-start(bf16[4,4,512]{2,1,0:T(4,128)(2,1)} %all_to_all.83), calls=%async_computation.4 | async-start | bytes 32768 | tf_op jit(solution)/shard_map/all_to_all | solution.py:65
  81.2 7.2 %all-to-all-start = ((bf16[4,4,2048]{2,1,0:T(4,128)(2,1)}), bf16[4,4,2048]{2,1,0:T(4,128)(2,1)S(1)}, u32[]{:S(2)}, u32[]{:S(2)}) async-start(bf16[4,4,2048]{2,1,0:T(4,128)(2,1)} %all_to_all.72), calls=%async_computation | async-start | bytes 131072 | tf_op jit(solution)/shard_map/all_to_all | solution.py:64
  88.5 23.6 %all-to-all-start.3 = ((bf16[4,4,2048]{2,1,0:T(4,128)(2,1)}), bf16[4,4,2048]{2,1,0:T(4,128)(2,1)S(1)}, u32[]{:S(2)}, u32[]{:S(2)}) async-start(bf16[4,4,2048]{2,1,0:T(4,128)(2,1)} %all_to_all.81), calls=%async_computation.3 | async-start | bytes 131072 | tf_op jit(solution)/shard_map/all_to_all | solution.py:64
  92.6 110.5 %all-reduce.9.cloned.1.call-start = ((), (), s32[]{:S(2)}) async-start(), calls=%async_computation.6 | async-start | bytes 524288 | tf_op jit(solution)/shard_map/psum | solution.py:98
  112.4 6.7 %copy-start.2 = (f32[4,8,8,3072]{3,2,0,1:T(8,128)S(1)}, f32[4,8,8,3072]{3,2,0,1:T(8,128)}, u32[]{:S(2)}) copy-start(f32[4,8,8,3072]{3,2,0,1:T(8,128)} %get-tuple-element.53) | copy-start | bytes 9437188
  137.7 3.1 %copy-start.3 = (f32[4,8,8,3072]{3,2,0,1:T(8,128)S(1)}, f32[4,8,8,3072]{3,2,0,1:T(8,128)}, u32[]{:S(2)}) copy-start(f32[4,8,8,3072]{3,2,0,1:T(8,128)} %get-tuple-element.54) | copy-start | bytes 9437188
  204.9 8.7 %all-to-all-start.2 = ((bf16[4,4,2048]{2,0,1:T(4,128)(2,1)}), bf16[4,4,2048]{2,0,1:T(4,128)(2,1)S(1)}, u32[]{:S(2)}, u32[]{:S(2)}) async-start(bf16[4,4,2048]{2,0,1:T(4,128)(2,1)} %copy.180), calls=%async_computation.2 | async-start | bytes 131072 | tf_op jit(solution)/shard_map/all_to_all | solution.py:112
  213.5 7.4 %all-to-all-start.5 = ((bf16[4,4,2048]{2,0,1:T(4,128)(2,1)}), bf16[4,4,2048]{2,0,1:T(4,128)(2,1)S(1)}, u32[]{:S(2)}, u32[]{:S(2)}) async-start(bf16[4,4,2048]{2,0,1:T(4,128)(2,1)} %copy.197), calls=%async_computation.5 | async-start | bytes 131072 | tf_op jit(solution)/shard_map/all_to_all | solution.py:112
  217.7 44.0 %all-reduce.11.cloned.1.call-start = ((), (), s32[]{:S(2)}) async-start(), calls=%async_computation.7 | async-start | bytes 524288 | tf_op jit(solution)/shard_map/psum | solution.py:117
  262.6 0.7 copy-start.6
Sparse Core Ops, SparseCore 0:
  159.3 43.7 all-reduce.8
  231.9 29.7 all-reduce.10
where the time goes:
time: 274 us; the launch traced here: 270 us
  waiting for transfers between devices  84.3 us (31%)
  blocking collectives  67.7 us (25%)
  matrix products  44.1 us (16%)
  starting transfers between devices  29.6 us (11%)
  local copies, waits for them, and re-layouts  22.9 us (8%)
  between operations  13.8 us (5%)
  other arithmetic  7.74 us (3%)
    psum x1, waiting for transfers between devices, per_device(): lax.psum((jnp.sum(weights, axis=3), local_blend), 'tp')  43.9 us
    psum x1, waiting for transfers between devices, per_device(): summed_out = lax.psum(partial_out, 'sect')  29.9 us
    pmax x2, blocking collectives, per_device(): cache_top = lax.pmax(local_top, 'tp')  25.5 us
    psum x1, blocking collectives, per_device(): summed_query, summed_pair = lax.psum((part_query, part_pair), 'tp')  18.9 us
    unnamed x17, local copies, waits for them, and re-layouts  18.3 us
    psum x1, blocking collectives, per_device(): lax.psum((jnp.sum(weights, axis=3), local_blend), 'tp')  12.7 us
    dot_general x2, matrix products, per_device(): jnp.einsum('jghp,pgd->jghd', weights.astype(jnp.bfloat16), value_rows, pr...  12.3 us
    dot_general x2, matrix products, per_device(): jnp.einsum('jghd,pgd->jghp', query_rot, key_rows, preferred_element_type=...  12 us
  transfers between devices with their start and end apart: 8, of which 6 were waited for; matrix products, arithmetic and copies ran while one was open for 10% of the time, Pallas kernels for 0%

commit v1 on v0

v1 whole, which is shorter than its diff:
```python
import functools
import math

import jax
import jax.numpy as jnp
import numpy as np
from jax import lax
from jax.experimental import pallas as pl
from jax.experimental.pallas import tpu as pltpu
from jax.sharding import PartitionSpec as P

D = 8192
HEADS = 64
KV_HEADS = 8
HEAD_DIM = 128
PER_KV = HEADS // KV_HEADS
STEPS = 2
LANES = 128
MESH = pl.DeviceIdType.MESH
F32 = jnp.float32
BF16 = jnp.bfloat16


def pack(tiles):
    half = (len(tiles) + 1) // 2
    low = list(tiles[half:])
    if len(low) < half:
        low.append(jnp.zeros_like(tiles[0]))
    top = jnp.concatenate(tiles[:half], axis=1) if half > 1 else tiles[0]
    bottom = jnp.concatenate(low, axis=1) if half > 1 else low[0]
    return jnp.concatenate([top, bottom], axis=0).astype(BF16)


def unpack(packed, count):
    half = (count + 1) // 2
    wide = packed.astype(F32)
    return [
        wide[(i // half) * 8 : (i // half) * 8 + 8, (i % half) * LANES : (i % half + 1) * LANES]
        for i in range(count)
    ]


def kernel(
    cfg,
    perm_ref, len_ref, gain_ref, inv_ref, x_hbm, wq_hbm, wkv_hbm, wo_hbm, cache_hbm,
    out_hbm,
    x_v, wq_v, wkv_v, wo_v, kv_v, bias_v, fin_v, part_v,
    m1, r1, m2, r2, m3, r3, st, rst, m4, r4, m5, r5,
    load_sem, wq_sem, cache_sem, wo_sem,
    s1, e1, s2, e2, s3, e3, s3b, e3b, s4, e4, s5, e5, s6, e6,
):
    n, rows, req, req_dev, block = cfg["n"], cfg["rows"], cfg["req"], cfg["req_dev"], cfg["block"]
    qc, kc = cfg["qc"], cfg["kc"]
    pr, pc, csplit = cfg["pr"], cfg["pc"], cfg["csplit"]
    heads_per = HEADS // n
    total = block + LANES
    s = lax.axis_index("sect")
    t = lax.axis_index("tp")
    same = s == t

    def remote(src, dst, ssem, rsem, sect, tp):
        return pltpu.make_async_remote_copy(
            src_ref=src, dst_ref=dst, send_sem=ssem, recv_sem=rsem,
            device_id={"sect": sect, "tp": tp}, device_id_type=MESH,
        )

    x_copy = pltpu.make_async_copy(x_hbm, x_v, load_sem.at[0])
    x_copy.start()
    nq = cfg["nq"]
    qw = qc // nq
    wq_copies = [
        pltpu.make_async_copy(
            wq_hbm.at[:, pl.ds(i * qw, qw)], wq_v.at[:, pl.ds(i * qw, qw)], wq_sem.at[i]
        )
        for i in range(nq)
    ]
    wkv_copy = pltpu.make_async_copy(wkv_hbm, wkv_v, load_sem.at[1])
    for c in wq_copies:
        c.start()
    wkv_copy.start()
    nc = cfg["nc"]
    cw = block // nc
    cache_copies = [
        pltpu.make_async_copy(
            cache_hbm.at[0, pl.ds(i * cw, cw)], kv_v.at[pl.ds(i * cw, cw)], cache_sem.at[i]
        )
        for i in range(nc)
    ]
    wo_copies = [
        pltpu.make_async_copy(
            wo_hbm.at[:, pl.ds(c * pc, pc)], wo_v.at[:, pl.ds(c * pc, pc)], wo_sem.at[c]
        )
        for c in range(csplit)
    ]

    barrier = pltpu.get_barrier_semaphore()
    for i in range(1, n):
        pl.semaphore_signal(
            barrier, inc=1, device_id={"sect": s, "tp": lax.rem(t + i, n)}, device_id_type=MESH
        )
        pl.semaphore_signal(
            barrier, inc=1, device_id={"sect": lax.rem(s + i, n), "tp": t}, device_id_type=MESH
        )
        pl.semaphore_signal(
            barrier, inc=1, device_id={"sect": lax.rem(s + i, n), "tp": s}, device_id_type=MESH
        )

    @pl.when(jnp.logical_not(same))
    def _():
        pl.semaphore_signal(barrier, inc=1, device_id={"sect": s, "tp": s}, device_id_type=MESH)

    ri = lax.broadcasted_iota(jnp.int32, (rows, rows), 0)
    ci = lax.broadcasted_iota(jnp.int32, (rows, rows), 1)
    big = 4096

    def slot_code(idx):
        return (idx >> 3) * req_dev + (idx & (req_dev - 1)) + ((idx & 7) >= req_dev).astype(jnp.int32) * big

    by_col = jnp.zeros((rows, rows), jnp.int32)
    by_row = jnp.zeros((rows, rows), jnp.int32)
    for c in range(rows):
        code = perm_ref[c % req] + (c // req) * big
        by_col = jnp.where(ci == c, code, by_col)
        by_row = jnp.where(ri == c, code, by_row)
    select = (by_col == slot_code(ri)).astype(F32).astype(BF16)
    select_back = (by_row == slot_code(ci)).astype(F32).astype(BF16)

    x_copy.wait()
    xs = jnp.dot(select, x_v[...], preferred_element_type=F32)
    square = jnp.sum(xs * xs, axis=1, keepdims=True)
    scaled = (xs * gain_ref[...].astype(F32)).astype(BF16)

    r8 = lax.broadcasted_iota(jnp.int32, (8, LANES), 0)
    lane = lax.broadcasted_iota(jnp.int32, (8, LANES), 1)
    lens = [len_ref[0, j] for j in range(req_dev)]
    ends = []
    run = 0
    for j in range(req_dev):
        run = run + lens[j]
        ends.append(run)

    qparts = []
    for i in range(nq):
        wq_copies[i].wait()
        if i < nc:
            cache_copies[i].start()
        qparts.append(
            jnp.dot(scaled, wq_v[:, i * qw : (i + 1) * qw], preferred_element_type=F32)
        )
    for i in range(nq, nc):
        cache_copies[i].start()
    wkv_copy.wait()
    kpart = jnp.dot(scaled, wkv_v[...], preferred_element_type=F32)
    acc = jnp.concatenate(qparts + [kpart], axis=1)
    for c in wo_copies:
        c.start()

    hi = square.astype(BF16).astype(F32)
    lo = square - hi
    lane_r = lax.broadcasted_iota(jnp.int32, (rows, LANES), 1)
    sq_tile = jnp.where(lane_r < 64, hi, lo)
    nt = (qc + kc) // LANES
    for o in range(n):
        sl = slice(o * 8, o * 8 + 8)
        tiles = [acc[sl, i * LANES : (i + 1) * LANES] for i in range(nt)] + [sq_tile[sl]]
        m1[o] = pack(tiles)

    pl.semaphore_wait(barrier, 3 * (n - 1) + jnp.where(same, 0, 1))

    for i in range(1, n):
        to = lax.rem(t + i, n)
        remote(m1.at[to], r1.at[t], s1.at[i], e1.at[t], s, to).start()

    pos = (r8 >= req_dev).astype(jnp.int32)
    step_row = pos
    for j in range(req_dev):
        pos = pos + jnp.where((r8 & (req_dev - 1)) == j, lens[j], 0)
    angle = pos.astype(F32) * inv_ref[...]
    cosine = jnp.cos(angle)
    sine = jnp.sin(angle)
    sine = jnp.where(lane < HEAD_DIM // 2, -sine, sine)
    rj = lax.broadcasted_iota(jnp.int32, (8, total), 0) & (req_dev - 1)
    rk = (lax.broadcasted_iota(jnp.int32, (8, total), 0) >= req_dev).astype(jnp.int32)
    col = lax.broadcasted_iota(jnp.int32, (8, total), 1)
    first = t * block
    low_b = jnp.zeros((8, total), jnp.int32)
    high_b = jnp.zeros((8, total), jnp.int32)
    for j in range(req_dev):
        low_b = jnp.where(rj == j, ends[j] - lens[j] - first, low_b)
        high_b = jnp.where(rj == j, ends[j] - first, high_b)
    old_ok = (col >= low_b) & (col < high_b) & (col < block)
    nidx = col - block
    new_limit = jnp.where(t == 0, block + 8, block)
    new_ok = (
        (col >= block) & (col < new_limit) & ((nidx & (req_dev - 1)) == rj)
        & ((nidx >= req_dev).astype(jnp.int32) <= rk)
    )
    bias_v[...] = jnp.where(old_ok | new_ok, 0.0, -1e30)
    kv_v[block + 16 : total, :] = jnp.zeros((LANES - 16, 2 * KV_HEADS * HEAD_DIM), BF16)

    sums = unpack(m1[t], nt + 1)
    for i in range(1, n):
        src = lax.rem(t + i, n)
        remote(m1.at[src], r1.at[src], s1.at[i], e1.at[src], s, src).wait_recv()
        sums = [a + b for a, b in zip(sums, unpack(r1[src], nt + 1))]
    sq = sums[nt][:, 0:1] + sums[nt][:, 64:65]
    inv_rms = lax.rsqrt(sq * (1.0 / D) + 1e-05)
    m2[...] = pack([a * inv_rms for a in sums[:nt]])

    for i in range(1, n):
        to = lax.rem(t + i, n)
        remote(m2, r2.at[s], s2.at[i], e2.at[s], t, to).start()

    @pl.when(jnp.logical_not(same))
    def _():
        remote(m2, r2.at[s], s2.at[0], e2.at[s], t, t).start()

    @pl.when(same)
    def _():
        r2[s] = m2[...]

    for c in cache_copies:
        c.wait()
    for src in range(n):
        @pl.when(jnp.logical_not(same & (s == src)))
        def _():
            remote(m2, r2.at[src], s2.at[0], e2.at[src], t, t).wait_recv()

    tiles = [unpack(r2[src], nt) for src in range(n)]
    qt = qc // LANES
    kt = kc // LANES

    def q_tile(head):
        return tiles[head // qt][head % qt]

    def kv_tile(index):
        return tiles[index // kt][qt + index % kt]

    def rotate(a):
        return a * cosine + pltpu.roll(a, HEAD_DIM // 2, 1) * sine

    factor = math.log2(math.e) / math.sqrt(HEAD_DIM)
    blends = []
    tops = []
    totals = []
    sent = 0
    zero8 = jnp.zeros((8, LANES), F32)
    for g in range(KV_HEADS):
        kcol = slice(g * 256, g * 256 + 128)
        vcol = slice(g * 256 + 128, g * 256 + 256)
        kv_v[block : block + 16, kcol] = jnp.concatenate(
            [rotate(kv_tile(2 * g)), zero8], axis=0
        ).astype(BF16)
        kv_v[block : block + 16, vcol] = jnp.concatenate(
            [kv_tile(2 * g + 1), zero8], axis=0
        ).astype(BF16)
        q = jnp.concatenate(
            [rotate(q_tile(g * PER_KV + h)) for h in range(PER_KV)], axis=0
        ).astype(BF16)
        sc = lax.dot_general(
            q, kv_v[:, kcol], (((1,), (1,)), ((), ())), preferred_element_type=F32
        )
        sc = sc.reshape(PER_KV, 8, total) * factor + bias_v[...][None]
        top = jnp.maximum(jnp.max(sc, axis=2, keepdims=True), -1e20)
        w = jnp.exp2(sc - top)
        tot = jnp.sum(w, axis=2, keepdims=True)
        o = jnp.dot(
            w.reshape(PER_KV * 8, total).astype(BF16), kv_v[:, vcol],
            preferred_element_type=F32,
        )
        for h in range(PER_KV):
            blends.append(o[h * 8 : h * 8 + 8])
            tops.append(top[h])
            totals.append(tot[h])
        while (sent + 1) * heads_per <= len(blends):
            d = sent
            hs = range(d * heads_per, (d + 1) * heads_per)
            m3[d] = pack([blends[h] for h in hs])
            stat = zero8
            for a, h in enumerate(hs):
                stat = jnp.where(lane == a, tops[h], stat)
                stat = jnp.where(lane == 64 + a, totals[h], stat)
            st[d] = stat

            @pl.when(t != d)
            def _():
                remote(st.at[d], rst.at[t], s3b.at[d], e3b.at[t], s, d).start()
                remote(m3.at[d], r3.at[t], s3.at[d], e3.at[t], s, d).start()

            sent += 1

    stats = [st[t]]
    for i in range(1, n):
        src = lax.rem(t + i, n)
        remote(st.at[src], rst.at[src], s3b.at[src], e3b.at[src], s, src).wait_recv()
        stats.append(rst[src])
    best = functools.reduce(jnp.maximum, stats)
    decay = [jnp.exp2(jnp.minimum(a - best, 0.0)) for a in stats]
    norm = sum(f * pltpu.roll(a, 64, 1) for f, a in zip(decay, stats))
    share = [f / norm for f in decay]
    att = [a * share[0][:, i : i + 1] for i, a in enumerate(unpack(m3[t], heads_per))]
    for i in range(1, n):
        src = lax.rem(t + i, n)
        remote(m3.at[src], r3.at[src], s3.at[src], e3.at[src], s, src).wait_recv()
        att = [
            a + b * share[i][:, k : k + 1]
            for k, (a, b) in enumerate(zip(att, unpack(r3[src], heads_per)))
        ]
    m4[...] = pack(att)

    for i in range(1, n):
        to = lax.rem(t + i, n)
        remote(m4, r4.at[s], s4.at[i], e4.at[s], t, to).start()

    @pl.when(jnp.logical_not(same))
    def _():
        remote(m4, r4.at[s], s4.at[0], e4.at[s], t, t).start()

    @pl.when(same)
    def _():
        r4[s] = m4[...]

    for src in range(n):
        @pl.when(jnp.logical_not(same & (s == src)))
        def _():
            remote(m4, r4.at[src], s4.at[0], e4.at[src], t, t).wait_recv()

    attended = jnp.concatenate(
        [jnp.concatenate(unpack(r4[src], heads_per), axis=1) for src in range(n)], axis=0
    ).astype(BF16)
    attended = jnp.dot(select_back, attended, preferred_element_type=F32).astype(BF16)

    for c in range(csplit):
        wo_copies[c].wait()
        part = jnp.dot(attended, wo_v[:, c * pc : (c + 1) * pc], preferred_element_type=F32)
        for r in range(n // csplit):
            p = r * csplit + c
            piece = part[r * pr : (r + 1) * pr]
            part_v[p] = piece
            m5[p] = piece.astype(BF16)

            @pl.when(s != p)
            def _():
                remote(m5.at[p], r5.at[s], s5.at[p], e5.at[s], p, t).start()

    prow = pl.ds(pl.multiple_of((s // csplit) * pr, pr), pr)
    pcol = pl.ds(pl.multiple_of(lax.rem(s, csplit) * pc, pc), pc)
    result = part_v[s] + x_v[prow, pcol].astype(F32)
    for i in range(1, n):
        src = lax.rem(s + i, n)
        remote(m5.at[src], r5.at[src], s5.at[src], e5.at[src], src, t).wait_recv()
        result = result + r5[src].astype(F32)
    fin_v[...] = result.astype(BF16)
    mine = out_hbm.at[prow, pcol]
    for i in range(1, n):
        remote(fin_v, mine, s6.at[i], e6.at[s], lax.rem(s + i, n), t).start()
    own = pltpu.make_async_copy(fin_v, mine, load_sem.at[2])
    own.start()

    for i in range(1, n):
        to = lax.rem(t + i, n)
        remote(m1.at[to], r1.at[t], s1.at[i], e1.at[t], s, to).wait_send()
        remote(m2, r2.at[s], s2.at[i], e2.at[s], t, to).wait_send()
        remote(m4, r4.at[s], s4.at[i], e4.at[s], t, to).wait_send()
        remote(m3.at[to], r3.at[t], s3.at[to], e3.at[t], s, to).wait_send()
        remote(st.at[to], rst.at[t], s3b.at[to], e3b.at[t], s, to).wait_send()
        across = lax.rem(s + i, n)
        remote(m5.at[across], r5.at[s], s5.at[across], e5.at[s], across, t).wait_send()

    @pl.when(jnp.logical_not(same))
    def _():
        remote(m2, r2.at[s], s2.at[0], e2.at[s], t, t).wait_send()
        remote(m4, r4.at[s], s4.at[0], e4.at[s], t, t).wait_send()

    own.wait()
    for i in range(1, n):
        src = lax.rem(s + i, n)
        srow = pl.ds(pl.multiple_of((src // csplit) * pr, pr), pr)
        scol = pl.ds(pl.multiple_of(lax.rem(src, csplit) * pc, pc), pc)
        remote(fin_v, mine, s6.at[i], e6.at[s], src, t).wait_send()
        remote(fin_v, out_hbm.at[srow, scol], s6.at[i], e6.at[src], src, t).wait_recv()


def per_device(n, tokens, gain, w_query, w_kv, w_out, cache, lengths, perm):
    steps, req, feat = tokens.shape
    rows = steps * req
    req_dev = lengths.shape[1]
    block = cache.shape[1]
    qc, kc = w_query.shape[1], w_kv.shape[1]
    cols = w_out.shape[1]
    csplit = min(n, cols // LANES)
    pr, pc = rows // (n // csplit), cols // csplit
    heads_per = HEADS // n
    nt = (qc + kc) // LANES
    assert steps == STEPS and steps * req_dev == 8 and req == n * req_dev
    cfg = dict(
        n=n, rows=rows, req=req, req_dev=req_dev, block=block, qc=qc, kc=kc,
        csplit=csplit, pr=pr, pc=pc, nq=max(1, qc // 512), nc=4,
    )
    w1 = (nt + 2) // 2 * LANES
    w2 = (nt + 1) // 2 * LANES
    w3 = (heads_per + 1) // 2 * LANES
    inv = np.exp(-(2.0 * np.arange(64) / HEAD_DIM) * math.log(500000.0)).astype(np.float32)
    inv = jnp.asarray(np.concatenate([inv, inv])[None])
    any_spec = pl.BlockSpec(memory_space=pl.ANY)
    smem = pl.BlockSpec(memory_space=pltpu.SMEM)
    vmem = pl.BlockSpec(memory_space=pltpu.VMEM)
    dma = pltpu.SemaphoreType.DMA
    out = pl.pallas_call(
        functools.partial(kernel, cfg),
        out_shape=jax.ShapeDtypeStruct((rows, cols), BF16),
        in_specs=[smem, smem, vmem, vmem] + [any_spec] * 5,
        out_specs=any_spec,
        scratch_shapes=[
            pltpu.VMEM((rows, feat), BF16),
            pltpu.VMEM(w_query.shape, BF16),
            pltpu.VMEM(w_kv.shape, BF16),
            pltpu.VMEM(w_out.shape, BF16),
            pltpu.VMEM((block + LANES, cache.shape[2]), BF16),
            pltpu.VMEM((8, block + LANES), F32),
            pltpu.VMEM((pr, pc), BF16),
            pltpu.VMEM((n, pr, pc), F32),
            pltpu.VMEM((n, 16, w1), BF16),
            pltpu.VMEM((n, 16, w1), BF16),
            pltpu.VMEM((16, w2), BF16),
            pltpu.VMEM((n, 16, w2), BF16),
            pltpu.VMEM((n, 16, w3), BF16),
            pltpu.VMEM((n, 16, w3), BF16),
            pltpu.VMEM((n, 8, LANES), F32),
            pltpu.VMEM((n, 8, LANES), F32),
            pltpu.VMEM((16, w3), BF16),
            pltpu.VMEM((n, 16, w3), BF16),
            pltpu.VMEM((n, pr, pc), BF16),
            pltpu.VMEM((n, pr, pc), BF16),
            dma((3,)),
            dma((cfg["nq"],)),
            dma((cfg["nc"],)),
            dma((csplit,)),
        ]
        + [dma((n,)) for _ in range(14)],
        compiler_params=pltpu.CompilerParams(
            collective_id=0, has_side_effects=True, vmem_limit_bytes=56 * 1024 * 1024
        ),
        cost_estimate=pl.CostEstimate(
            flops=2 * rows * feat * (qc + kc + cols) + 4 * 64 * block * 8 * 128,
            bytes_accessed=2 * (feat * (qc + kc) + w_out.size + cache.size),
            transcendentals=64 * 8 * block,
        ),
    )(
        perm, lengths, gain.reshape(1, feat), inv,
        tokens.reshape(rows, feat), w_query, w_kv, w_out, cache,
    )
    return out.reshape(steps, req, cols)


def solution(mesh):
    n = mesh.shape["sect"]
    assert mesh.shape["tp"] == n
    return jax.shard_map(
        functools.partial(per_device, n),
        mesh=mesh,
        in_specs=(
            P(None, "groups", "tp"),
            P("tp"),
            P("tp", "sect"),
            P("tp", "sect"),
            P("sect", "tp"),
            P(("groups", "sect"), "tp", None),
            P(("groups", "sect"), None),
            P("groups"),
        ),
        out_specs=P(None, "groups", "tp"),
        check_vma=False,
    )
```

time: 274 us -> 43.3 us (0.16); the launches traced: 270 us -> 42.8 us
  waiting for transfers between devices: 84.3 us -> 0 us
  blocking collectives: 67.7 us -> 0 us
  matrix products: 44.1 us -> 0 us
  Pallas kernels: 0 us -> 39.9 us
  starting transfers between devices: 29.6 us -> 0 us
  local copies, waits for them, and re-layouts: 22.9 us -> 2.86 us
  between operations: 13.8 us -> 0.01 us
  other arithmetic: 7.74 us -> 0 us
    psum x2 -> x0, waiting for transfers between devices: 73.7 us -> none  [the longest x1 43.9 us: per_device(): lax.psum((jnp.sum(weights, axis=3), local_blend), 'tp')]
    dot_general x17 -> x0, matrix products: 44.1 us -> none  [the longest x2 12.3 us: per_device(): jnp.einsum('jghp,pgd->jghd', weights.astype(jnp.bfloat16), value_rows, pr...]
    psum x3 -> x0, blocking collectives: 42.3 us -> none  [the longest x1 18.9 us: per_device(): summed_query, summed_pair = lax.psum((part_query, part_pair), 'tp')]
    pallas_call x0 -> x1, Pallas kernels: none -> 39.9 us  [per_device(): pl.pallas_call(functools.partial(kernel, cfg), out_shape=jax.ShapeDtypeSt...]
    all_to_all x6 -> x0, starting transfers between devices: 29.6 us -> none  [the longest x2 11.9 us: per_device(): lax.all_to_all(pair_slot, 'sect', split_axis=0, concat_axis=1, tiled=True)]
    pmax x2 -> x0, blocking collectives: 25.5 us -> none  [per_device(): cache_top = lax.pmax(local_top, 'tp')]
    unnamed x17 -> x1, local copies, waits for them, and re-layouts: 18.3 us -> 1.57 us
    all_to_all x6 -> x0, waiting for transfers between devices: 10.6 us -> none  [the longest x2 4.63 us: per_device(): lax.all_to_all(attended, 'sect', split_axis=1, concat_axis=0, tiled=True)]
  transfers between devices with their start and end apart: 8 -> 0, of which waited for: 6 -> 0; matrix products, arithmetic and copies ran while one was open for 10% -> 0% of each run, Pallas kernels for 0% -> 0%
where the time goes in v1:
time: 43.3 us; the launch traced here: 42.8 us
  Pallas kernels  39.9 us (92%)
  local copies, waits for them, and re-layouts  2.86 us (7%)
    pallas_call x1, Pallas kernels, per_device(): pl.pallas_call(functools.partial(kernel, cfg), out_shape=jax.ShapeDtypeSt...  39.9 us
    unnamed x1, local copies, waits for them, and re-layouts  1.57 us
    reshape x1, local copies, waits for them, and re-layouts, per_device(): gain.reshape(1, feat)  1.29 us

profile of v1, /device:TPU:1, one launch (start us, length us, event | category | flops | bytes accessed | tf_op | source)
XLA Modules:
  0.0 42.8 jit_solution(13039535114270094721)
XLA Ops:
  0.0 1.3 %reshape.9.gain_ref = bf16[1,2048]{1,0:T(2,128)(2,1)} reshape(bf16[2048]{0:T(1024)(128)(2,1)} %param.10) | data formatting | bytes 8192 | tf_op jit(solution)/shard_map/reshape | solution.py:450
  1.3 39.9 %shard_map.91 = bf16[32,2048]{1,0:T(8,128)(2,1)} custom-call(s32[16]{0:T(128)} %perm_ref.1, s32[1,4]{1,0:T(1,128)} %len_ref.1, bf16[1,2048]{1,0:T(2,128)(2,1)} %reshape.9.gain_ref, f32[1,128]{1,0:T(1,128)} %constant.2.clone.inv_ref, bf16[32,2048]{1,0:T(8,128)(2,1)} %bitcast.3, bf16[2048,2048]{1,0:T(8,128)(2,1)} %wq_hbm.1, bf16[2048,512]{1,0:T(8,128)(2,1)} %wkv_hbm.1, ...), custom_call_target="tpu_custom_call" | custom-call | flops 1409286144 | bytes 31457280 | tf_op jit(solution)/shard_map/pallas_call | solution.py:409
  41.2 1.6 %copy.11 = bf16[2,16,2048]{2,1,0:T(8,128)(2,1)} copy(bf16[2,16,2048]{2,1,0:T(8,128)(2,1)} %bitcast.2) | data formatting | bytes 262144

commit v2 on v1

v2 whole, which is shorter than its diff:
```python
import functools
import math

import jax
import jax.numpy as jnp
import numpy as np
from jax import lax
from jax.experimental import pallas as pl
from jax.experimental.pallas import tpu as pltpu
from jax.sharding import PartitionSpec as P

D = 8192
HEADS = 64
KV_HEADS = 8
HEAD_DIM = 128
PER_KV = HEADS // KV_HEADS
STEPS = 2
LANES = 128
MESH = pl.DeviceIdType.MESH
F32 = jnp.float32
BF16 = jnp.bfloat16


def pack(tiles):
    half = (len(tiles) + 1) // 2
    low = list(tiles[half:])
    if len(low) < half:
        low.append(jnp.zeros_like(tiles[0]))
    top = jnp.concatenate(tiles[:half], axis=1) if half > 1 else tiles[0]
    bottom = jnp.concatenate(low, axis=1) if half > 1 else low[0]
    return jnp.concatenate([top, bottom], axis=0).astype(BF16)


def unpack(packed, count):
    half = (count + 1) // 2
    wide = packed.astype(F32)
    return [
        wide[(i // half) * 8 : (i // half) * 8 + 8, (i % half) * LANES : (i % half + 1) * LANES]
        for i in range(count)
    ]


def kernel(
    cfg,
    perm_ref, len_ref, gain_ref, inv_ref, x_hbm, wq_hbm, wkv_hbm, wo_hbm, cache_hbm,
    out_hbm,
    x_v, wq_v, wkv_v, wo_v, kv_v, bias_v, fin_v,
    m1, r1, m2, r2, m3, r3, st, rst, m4, r4, m5, r5,
    load_sem, wq_sem, cache_sem, wo_sem, out_sem,
    s1, e1, s2, e2, s3, e3, s3b, e3b, s4, e4, s5, e5,
):
    n, rows, req, req_dev, block = cfg["n"], cfg["rows"], cfg["req"], cfg["req_dev"], cfg["block"]
    qc, kc, nq, unit, nu = cfg["qc"], cfg["kc"], cfg["nq"], cfg["unit"], cfg["nu"]
    nch, cw = cfg["nch"], cfg["cw"]
    heads_per = HEADS // n
    total = block + LANES
    s = lax.axis_index("sect")
    t = lax.axis_index("tp")
    same = s == t

    def remote(src, dst, ssem, rsem, sect, tp):
        return pltpu.make_async_remote_copy(
            src_ref=src, dst_ref=dst, send_sem=ssem, recv_sem=rsem,
            device_id={"sect": sect, "tp": tp}, device_id_type=MESH,
        )

    x_copy = pltpu.make_async_copy(x_hbm, x_v, load_sem.at[0])
    x_copy.start()
    wkv_copy = pltpu.make_async_copy(wkv_hbm, wkv_v, load_sem.at[1])
    wkv_copy.start()
    qw = qc // nq
    wq_copies = [
        pltpu.make_async_copy(
            wq_hbm.at[:, pl.ds(i * qw, qw)], wq_v.at[:, pl.ds(i * qw, qw)], wq_sem.at[i]
        )
        for i in range(nq)
    ]
    for c in wq_copies:
        c.start()
    nc = cfg["nc"]
    crows = block // nc
    cache_copies = [
        pltpu.make_async_copy(
            cache_hbm.at[0, pl.ds(i * crows, crows)],
            kv_v.at[pl.ds(i * crows, crows)],
            cache_sem.at[i],
        )
        for i in range(nc)
    ]
    uw = unit * HEAD_DIM
    wo_copies = [
        pltpu.make_async_copy(wo_hbm.at[pl.ds(u * uw, uw)], wo_v.at[pl.ds(u * uw, uw)], wo_sem.at[u])
        for u in range(nu)
    ]

    barrier = pltpu.get_barrier_semaphore()
    for i in range(1, n):
        pl.semaphore_signal(
            barrier, inc=1, device_id={"sect": s, "tp": lax.rem(t + i, n)}, device_id_type=MESH
        )
        pl.semaphore_signal(
            barrier, inc=1, device_id={"sect": lax.rem(s + i, n), "tp": t}, device_id_type=MESH
        )
        pl.semaphore_signal(
            barrier, inc=1, device_id={"sect": lax.rem(s + i, n), "tp": s}, device_id_type=MESH
        )

    @pl.when(jnp.logical_not(same))
    def _():
        pl.semaphore_signal(barrier, inc=1, device_id={"sect": s, "tp": s}, device_id_type=MESH)

    ri = lax.broadcasted_iota(jnp.int32, (rows, rows), 0)
    ci = lax.broadcasted_iota(jnp.int32, (rows, rows), 1)
    big = 4096

    def slot_code(idx):
        return (idx >> 3) * req_dev + (idx & (req_dev - 1)) + ((idx & 7) >= req_dev).astype(jnp.int32) * big

    by_col = jnp.zeros((rows, rows), jnp.int32)
    by_row = jnp.zeros((rows, rows), jnp.int32)
    for c in range(rows):
        code = perm_ref[c % req] + (c // req) * big
        by_col = jnp.where(ci == c, code, by_col)
        by_row = jnp.where(ri == c, code, by_row)
    select = (by_col == slot_code(ri)).astype(F32).astype(BF16)
    select_back = (by_row == slot_code(ci)).astype(F32).astype(BF16)

    x_copy.wait()
    xs = jnp.dot(select, x_v[...], preferred_element_type=F32)
    square = jnp.sum(xs * xs, axis=1, keepdims=True)
    scaled = (xs * gain_ref[...].astype(F32).reshape(1, -1)).astype(BF16)

    r8 = lax.broadcasted_iota(jnp.int32, (8, LANES), 0)
    lane = lax.broadcasted_iota(jnp.int32, (8, LANES), 1)
    lens = [len_ref[0, j] for j in range(req_dev)]
    ends = []
    run = 0
    for j in range(req_dev):
        run = run + lens[j]
        ends.append(run)

    hi = square.astype(BF16).astype(F32)
    lo = square - hi
    lane_r = lax.broadcasted_iota(jnp.int32, (rows, LANES), 1)
    sq_tile = jnp.where(lane_r < 64, hi, lo)
    qt = qw // LANES
    kt = kc // LANES
    counts = [qt + (kt if h == 0 else 0) for h in range(nq)]
    w1 = [pl.ds(0, (counts[h] + (h == 0) + 1) // 2 * LANES) for h in range(nq)]
    w2 = [pl.ds(0, (counts[h] + 1) // 2 * LANES) for h in range(nq)]

    def tile_rows(array, o):
        return [
            array[o * 8 : o * 8 + 8, i * LANES : (i + 1) * LANES]
            for i in range(array.shape[1] // LANES)
        ]

    wkv_copy.wait()
    kpart = jnp.dot(scaled, wkv_v[...], preferred_element_type=F32)
    for h in range(nq):
        wq_copies[h].wait()
        if h == nq - 1:
            for c in cache_copies:
                c.start()
            for c in wo_copies:
                c.start()
        qpart = jnp.dot(scaled, wq_v[:, h * qw : (h + 1) * qw], preferred_element_type=F32)
        for o in range(n):
            tiles = tile_rows(qpart, o)
            if h == 0:
                tiles = tile_rows(kpart, o) + tiles + [sq_tile[o * 8 : o * 8 + 8]]
            m1[h, o, :, w1[h]] = pack(tiles)
        if h == 0:
            pl.semaphore_wait(barrier, 3 * (n - 1) + jnp.where(same, 0, 1))
        for i in range(1, n):
            to = lax.rem(t + i, n)
            remote(
                m1.at[h, to, :, w1[h]], r1.at[h, t, :, w1[h]], s1.at[h, i], e1.at[h, t], s, to
            ).start()

    pos = (r8 >= req_dev).astype(jnp.int32)
    step_row = pos
    for j in range(req_dev):
        pos = pos + jnp.where((r8 & (req_dev - 1)) == j, lens[j], 0)
    angle = pos.astype(F32) * inv_ref[...]
    cosine = jnp.cos(angle)
    sine = jnp.sin(angle)
    sine = jnp.where(lane < HEAD_DIM // 2, -sine, sine)
    rj = lax.broadcasted_iota(jnp.int32, (8, total), 0) & (req_dev - 1)
    rk = (lax.broadcasted_iota(jnp.int32, (8, total), 0) >= req_dev).astype(jnp.int32)
    col = lax.broadcasted_iota(jnp.int32, (8, total), 1)
    first = t * block
    low_b = jnp.zeros((8, total), jnp.int32)
    high_b = jnp.zeros((8, total), jnp.int32)
    for j in range(req_dev):
        low_b = jnp.where(rj == j, ends[j] - lens[j] - first, low_b)
        high_b = jnp.where(rj == j, ends[j] - first, high_b)
    old_ok = (col >= low_b) & (col < high_b) & (col < block)
    nidx = col - block
    new_limit = jnp.where(t == 0, block + 8, block)
    new_ok = (
        (col >= block) & (col < new_limit) & ((nidx & (req_dev - 1)) == rj)
        & ((nidx >= req_dev).astype(jnp.int32) <= rk)
    )
    bias_v[...] = jnp.where(old_ok | new_ok, 0.0, -1e30)
    kv_v[block + 16 : total, :] = jnp.zeros((LANES - 16, 2 * KV_HEADS * HEAD_DIM), BF16)

    inv_rms = None
    for h in range(nq):
        count = counts[h] + (h == 0)
        sums = unpack(m1[h, t, :, w1[h]], count)
        for i in range(1, n):
            src = lax.rem(t + i, n)
            remote(
                m1.at[h, src, :, w1[h]], r1.at[h, src, :, w1[h]], s1.at[h, i], e1.at[h, src], s, src
            ).wait_recv()
            sums = [a + b for a, b in zip(sums, unpack(r1[h, src, :, w1[h]], count))]
        if h == 0:
            sq = sums[-1][:, 0:1] + sums[-1][:, 64:65]
            inv_rms = lax.rsqrt(sq * (1.0 / D) + 1e-05)
            sums = sums[:-1]
        m2[h, :, w2[h]] = pack([a * inv_rms for a in sums])
        for i in range(1, n):
            to = lax.rem(t + i, n)
            remote(
                m2.at[h, :, w2[h]], r2.at[h, s, :, w2[h]], s2.at[h, i], e2.at[h, s], t, to
            ).start()

        @pl.when(jnp.logical_not(same))
        def _():
            remote(
                m2.at[h, :, w2[h]], r2.at[h, s, :, w2[h]], s2.at[h, 0], e2.at[h, s], t, t
            ).start()

        @pl.when(same)
        def _():
            r2[h, s, :, w2[h]] = m2[h, :, w2[h]]

    for c in cache_copies:
        c.wait()
    held = {}

    def routed(src, h):
        if (src, h) not in held:
            @pl.when(jnp.logical_not(same & (s == src)))
            def _():
                remote(
                    m2.at[h, :, w2[h]], r2.at[h, src, :, w2[h]], s2.at[h, 0], e2.at[h, src], t, t
                ).wait_recv()

            held[src, h] = unpack(r2[h, src, :, w2[h]], counts[h])
        return held[src, h]

    per_src = nq * qt

    def q_tile(head):
        src, inner = head // per_src, head % per_src
        return routed(src, inner // qt)[(kt if inner // qt == 0 else 0) + inner % qt]

    def kv_tile(index):
        return routed(index // kt, 0)[index % kt]

    def rotate(a):
        return a * cosine + pltpu.roll(a, HEAD_DIM // 2, 1) * sine

    def last_part(g):
        return max((head % per_src) // qt for head in range(g * PER_KV, (g + 1) * PER_KV))

    factor = math.log2(math.e) / math.sqrt(HEAD_DIM)
    zero8 = jnp.zeros((8, LANES), F32)
    for g in sorted(range(KV_HEADS), key=lambda g: (last_part(g), g)):
        kcol = slice(g * 256, g * 256 + 128)
        vcol = slice(g * 256 + 128, g * 256 + 256)
        kv_v[block : block + 16, kcol] = jnp.concatenate(
            [rotate(kv_tile(2 * g)), zero8], axis=0
        ).astype(BF16)
        kv_v[block : block + 16, vcol] = jnp.concatenate(
            [kv_tile(2 * g + 1), zero8], axis=0
        ).astype(BF16)
        q = jnp.concatenate(
            [rotate(q_tile(g * PER_KV + h)) for h in range(PER_KV)], axis=0
        ).astype(BF16)
        sc = lax.dot_general(
            q, kv_v[:, kcol], (((1,), (1,)), ((), ())), preferred_element_type=F32
        )
        sc = sc.reshape(PER_KV, 8, total) * factor + bias_v[...][None]
        top = jnp.maximum(jnp.max(sc, axis=2, keepdims=True), -1e20)
        w = jnp.exp2(sc - top)
        tot = jnp.sum(w, axis=2, keepdims=True)
        o = jnp.dot(
            w.reshape(PER_KV * 8, total).astype(BF16), kv_v[:, vcol],
            preferred_element_type=F32,
        )
        for first_head in range(0, PER_KV, unit):
            head = g * PER_KV + first_head
            d, u = head // heads_per, (head % heads_per) // unit
            hs = range(first_head, first_head + unit)
            m3[u, d] = pack([o[h * 8 : h * 8 + 8] for h in hs])
            stat = zero8
            for a, h in enumerate(hs):
                stat = jnp.where(lane == a, top[h], stat)
                stat = jnp.where(lane == 64 + a, tot[h], stat)
            st[u, d] = stat

            @pl.when(t != d)
            def _():
                remote(st.at[u, d], rst.at[u, t], s3b.at[u, d], e3b.at[u, t], s, d).start()
                remote(m3.at[u, d], r3.at[u, t], s3.at[u, d], e3.at[u, t], s, d).start()

    for u in range(nu):
        stats = [st[u, t]]
        for i in range(1, n):
            src = lax.rem(t + i, n)
            remote(
                st.at[u, src], rst.at[u, src], s3b.at[u, src], e3b.at[u, src], s, src
            ).wait_recv()
            stats.append(rst[u, src])
        best = functools.reduce(jnp.maximum, stats)
        decay = [jnp.exp2(jnp.minimum(a - best, 0.0)) for a in stats]
        norm = sum(f * pltpu.roll(a, 64, 1) for f, a in zip(decay, stats))
        share = [f / norm for f in decay]
        att = [a * share[0][:, i : i + 1] for i, a in enumerate(unpack(m3[u, t], unit))]
        for i in range(1, n):
            src = lax.rem(t + i, n)
            remote(m3.at[u, src], r3.at[u, src], s3.at[u, src], e3.at[u, src], s, src).wait_recv()
            att = [
                a + b * share[i][:, k : k + 1]
                for k, (a, b) in enumerate(zip(att, unpack(r3[u, src], unit)))
            ]
        m4[u] = pack(att)
        for i in range(1, n):
            to = lax.rem(t + i, n)
            remote(m4.at[u], r4.at[u, s], s4.at[u, i], e4.at[u, s], t, to).start()

        @pl.when(jnp.logical_not(same))
        def _():
            remote(m4.at[u], r4.at[u, s], s4.at[u, 0], e4.at[u, s], t, t).start()

        @pl.when(same)
        def _():
            r4[u, s] = m4[u]

    lefts = []
    for u in range(nu):
        for src in range(n):
            @pl.when(jnp.logical_not(same & (s == src)))
            def _():
                remote(m4.at[u], r4.at[u, src], s4.at[u, 0], e4.at[u, src], t, t).wait_recv()

        attended = jnp.concatenate(
            [jnp.concatenate(unpack(r4[u, src], unit), axis=1) for src in range(n)], axis=0
        ).astype(BF16)
        lefts.append(jnp.dot(select_back, attended, preferred_element_type=F32).astype(BF16))
        wo_copies[u].wait()
        if u < nu - 1:
            early = jnp.dot(lefts[u], wo_v[u * uw : (u + 1) * uw, :], preferred_element_type=F32)
            fin_v[...] = early if u == 0 else fin_v[...] + early

    u = nu - 1
    for c in range(nch):
        ccol = slice(c * cw, (c + 1) * cw)
        part = jnp.dot(lefts[u], wo_v[u * uw : (u + 1) * uw, ccol], preferred_element_type=F32)
        if nu > 1:
            part = part + fin_v[:, ccol]
        m5[c] = part.astype(BF16)
        for i in range(1, n):
            to = lax.rem(s + i, n)
            remote(m5.at[c], r5.at[c, s], s5.at[c, i], e5.at[c, s], to, t).start()
        r5[c, s] = m5[c]

    for i in range(1, n):
        to = lax.rem(t + i, n)
        for h in range(nq):
            remote(
                m1.at[h, to, :, w1[h]], r1.at[h, t, :, w1[h]], s1.at[h, i], e1.at[h, t], s, to
            ).wait_send()
            remote(
                m2.at[h, :, w2[h]], r2.at[h, s, :, w2[h]], s2.at[h, i], e2.at[h, s], t, to
            ).wait_send()
        for u in range(nu):
            remote(m4.at[u], r4.at[u, s], s4.at[u, i], e4.at[u, s], t, to).wait_send()
            remote(m3.at[u, to], r3.at[u, t], s3.at[u, to], e3.at[u, t], s, to).wait_send()
            remote(st.at[u, to], rst.at[u, t], s3b.at[u, to], e3b.at[u, t], s, to).wait_send()

    @pl.when(jnp.logical_not(same))
    def _():
        for h in range(nq):
            remote(
                m2.at[h, :, w2[h]], r2.at[h, s, :, w2[h]], s2.at[h, 0], e2.at[h, s], t, t
            ).wait_send()
        for u in range(nu):
            remote(m4.at[u], r4.at[u, s], s4.at[u, 0], e4.at[u, s], t, t).wait_send()

    outs = []
    for c in range(nch):
        ccol = slice(c * cw, (c + 1) * cw)
        for i in range(1, n):
            src = lax.rem(s + i, n)
            remote(m5.at[c], r5.at[c, src], s5.at[c, i], e5.at[c, src], src, t).wait_recv()
        result = x_v[:, ccol].astype(F32)
        for src in range(n):
            result = result + r5[c, src].astype(F32)
        x_v[:, ccol] = result.astype(BF16)
        outs.append(
            pltpu.make_async_copy(x_v.at[:, ccol], out_hbm.at[:, ccol], out_sem.at[c])
        )
        outs[c].start()
    for c in range(nch):
        for i in range(1, n):
            to = lax.rem(s + i, n)
            remote(m5.at[c], r5.at[c, s], s5.at[c, i], e5.at[c, s], to, t).wait_send()
        outs[c].wait()


def per_device(n, tokens, gain, w_query, w_kv, w_out, cache, lengths, perm):
    steps, req, feat = tokens.shape
    rows = steps * req
    req_dev = lengths.shape[1]
    block = cache.shape[1]
    qc, kc = w_query.shape[1], w_kv.shape[1]
    cols = w_out.shape[1]
    heads_per = HEADS // n
    unit = min(heads_per, PER_KV)
    nu = heads_per // unit
    nq = max(1, qc // 1024)
    nch = max(1, cols // 1024)
    cw = cols // nch
    assert steps == STEPS and steps * req_dev == 8 and req == n * req_dev
    cfg = dict(
        n=n, rows=rows, req=req, req_dev=req_dev, block=block, qc=qc, kc=kc,
        nq=nq, nc=4, unit=unit, nu=nu, nch=nch, cw=cw,
    )
    widest = qc // nq // LANES + kc // LANES
    w1 = (widest + 2) // 2 * LANES
    w2 = (widest + 1) // 2 * LANES
    w3 = (unit + 1) // 2 * LANES
    inv = np.exp(-(2.0 * np.arange(64) / HEAD_DIM) * math.log(500000.0)).astype(np.float32)
    inv = jnp.asarray(np.concatenate([inv, inv])[None])
    any_spec = pl.BlockSpec(memory_space=pl.ANY)
    smem = pl.BlockSpec(memory_space=pltpu.SMEM)
    vmem = pl.BlockSpec(memory_space=pltpu.VMEM)
    dma = pltpu.SemaphoreType.DMA
    out = pl.pallas_call(
        functools.partial(kernel, cfg),
        out_shape=jax.ShapeDtypeStruct((rows, cols), BF16),
        in_specs=[smem, smem, vmem, vmem] + [any_spec] * 5,
        out_specs=any_spec,
        scratch_shapes=[
            pltpu.VMEM((rows, feat), BF16),
            pltpu.VMEM(w_query.shape, BF16),
            pltpu.VMEM(w_kv.shape, BF16),
            pltpu.VMEM(w_out.shape, BF16),
            pltpu.VMEM((block + LANES, cache.shape[2]), BF16),
            pltpu.VMEM((8, block + LANES), F32),
            pltpu.VMEM((rows, cols), F32),
            pltpu.VMEM((nq, n, 16, w1), BF16),
            pltpu.VMEM((nq, n, 16, w1), BF16),
            pltpu.VMEM((nq, 16, w2), BF16),
            pltpu.VMEM((nq, n, 16, w2), BF16),
            pltpu.VMEM((nu, n, 16, w3), BF16),
            pltpu.VMEM((nu, n, 16, w3), BF16),
            pltpu.VMEM((nu, n, 8, LANES), F32),
            pltpu.VMEM((nu, n, 8, LANES), F32),
            pltpu.VMEM((nu, 16, w3), BF16),
            pltpu.VMEM((nu, n, 16, w3), BF16),
            pltpu.VMEM((nch, rows, cw), BF16),
            pltpu.VMEM((nch, n, rows, cw), BF16),
            dma((2,)),
            dma((nq,)),
            dma((cfg["nc"],)),
            dma((nu,)),
            dma((nch,)),
        ]
        + [dma((nq, n))] * 4
        + [dma((nu, n))] * 6
        + [dma((nch, n))] * 2,
        compiler_params=pltpu.CompilerParams(
            collective_id=0, has_side_effects=True, vmem_limit_bytes=56 * 1024 * 1024
        ),
        cost_estimate=pl.CostEstimate(
            flops=2 * rows * feat * (qc + kc + cols) + 4 * 64 * block * 8 * 128,
            bytes_accessed=2 * (feat * (qc + kc) + w_out.size + cache.size),
            transcendentals=64 * 8 * block,
        ),
    )(
        perm, lengths, gain, inv,
        tokens.reshape(rows, feat), w_query, w_kv, w_out, cache,
    )
    return out.reshape(steps, req, cols)


def solution(mesh):
    n = mesh.shape["sect"]
    assert mesh.shape["tp"] == n
    return jax.shard_map(
        functools.partial(per_device, n),
        mesh=mesh,
        in_specs=(
            P(None, "groups", "tp"),
            P("tp"),
            P("tp", "sect"),
            P("tp", "sect"),
            P("sect", "tp"),
            P(("groups", "sect"), "tp", None),
            P(("groups", "sect"), None),
            P("groups"),
        ),
        out_specs=P(None, "groups", "tp"),
        check_vma=False,
    )
```

time: 43.3 us -> 42.1 us (0.972)
  local copies, waits for them, and re-layouts: 2.86 us -> 1.57 us
    reshape x1 -> x0, local copies, waits for them, and re-layouts: 1.29 us -> none  [per_device(): gain.reshape(1, feat)]
where the time goes in v2:
time: 42.1 us; the launch traced here: 41.9 us
  Pallas kernels  40.3 us (96%)
  local copies, waits for them, and re-layouts  1.57 us (4%)
    pallas_call x1, Pallas kernels, per_device(): pl.pallas_call(functools.partial(kernel, cfg), out_shape=jax.ShapeDtypeSt...  40.3 us
    unnamed x1, local copies, waits for them, and re-layouts  1.57 us

profile of v2, /device:TPU:1, one launch (start us, length us, event | category | flops | bytes accessed | tf_op | source)
XLA Modules:
  0.0 41.9 jit_solution(4690111739956688704)
XLA Ops:
  0.0 40.3 %shard_map.91 = bf16[32,2048]{1,0:T(8,128)(2,1)} custom-call(s32[16]{0:T(128)} %perm_ref.1, s32[1,4]{1,0:T(1,128)} %len_ref.1, bf16[2048]{0:T(1024)(128)(2,1)} %gain_ref.1, f32[1,128]{1,0:T(1,128)} %constant.2.clone.inv_ref, bf16[32,2048]{1,0:T(8,128)(2,1)} %bitcast.3, bf16[2048,2048]{1,0:T(8,128)(2,1)} %wq_hbm.1, bf16[2048,512]{1,0:T(8,128)(2,1)} %wkv_hbm.1, ...), custom_call_target="tpu_custom_call" | custom-call | flops 1409286144 | bytes 31457280 | tf_op jit(solution)/shard_map/pallas_call | solution.py:443
  40.4 1.6 %copy.11 = bf16[2,16,2048]{2,1,0:T(8,128)(2,1)} copy(bf16[2,16,2048]{2,1,0:T(8,128)(2,1)} %bitcast.2) | data formatting | bytes 262144

commit v3 on v2

--- a/solution.py
+++ b/solution.py
@@ -44,14 +44,14 @@
     cfg,
     perm_ref, len_ref, gain_ref, inv_ref, x_hbm, wq_hbm, wkv_hbm, wo_hbm, cache_hbm,
     out_hbm,
-    x_v, wq_v, wkv_v, wo_v, kv_v, bias_v, fin_v,
-    m1, r1, m2, r2, m3, r3, st, rst, m4, r4, m5, r5,
-    load_sem, wq_sem, cache_sem, wo_sem, out_sem,
-    s1, e1, s2, e2, s3, e3, s3b, e3b, s4, e4, s5, e5,
+    x_v, wq_v, wkv_v, wo_v, kv_v, bias_v, fin_v, part_v,
+    m1, r1, m2, r2, m3, r3, st, rst, m4, r4, m5, r5, m6,
+    load_sem, wq_sem, cache_sem, wo_sem,
+    s1, e1, s2, e2, s3, e3, s3b, e3b, s4, e4, s5, e5, s6, e6,
 ):
     n, rows, req, req_dev, block = cfg["n"], cfg["rows"], cfg["req"], cfg["req_dev"], cfg["block"]
     qc, kc, nq, unit, nu = cfg["qc"], cfg["kc"], cfg["nq"], cfg["unit"], cfg["nu"]
-    nch, cw = cfg["nch"], cfg["cw"]
+    half = cfg["half"]
     heads_per = HEADS // n
     total = block + LANES
     s = lax.axis_index("sect")
@@ -356,17 +356,34 @@
             early = jnp.dot(lefts[u], wo_v[u * uw : (u + 1) * uw, :], preferred_element_type=F32)
             fin_v[...] = early if u == 0 else fin_v[...] + early
 
+    core = lax.rem(s, 2)
+    partner = s + 1 - 2 * core
     u = nu - 1
-    for c in range(nch):
-        ccol = slice(c * cw, (c + 1) * cw)
+    for c in range(2):
+        ccol = slice(c * half, (c + 1) * half)
         part = jnp.dot(lefts[u], wo_v[u * uw : (u + 1) * uw, ccol], preferred_element_type=F32)
         if nu > 1:
             part = part + fin_v[:, ccol]
-        m5[c] = part.astype(BF16)
-        for i in range(1, n):
-            to = lax.rem(s + i, n)
-            remote(m5.at[c], r5.at[c, s], s5.at[c, i], e5.at[c, s], to, t).start()
-        r5[c, s] = m5[c]
+        part_v[c] = part
+
+        @pl.when(core != c)
+        def _():
+            m5[...] = part.astype(BF16)
+            remote(m5, r5, s5.at[0], e5.at[0], partner, t).start()
+
+    remote(m5, r5, s5.at[0], e5.at[0], partner, t).wait_recv()
+    m6[...] = (part_v[core] + r5[...].astype(F32)).astype(BF16)
+
+    def landing(src):
+        return out_hbm.at[
+            src // 2, :, pl.ds(pl.multiple_of(lax.rem(src, 2) * half, half), half)
+        ]
+
+    order = sorted(range(1, n), key=lambda i: i % 2)
+    for i in order:
+        remote(m6, landing(s), s6.at[i], e6.at[s], lax.rem(s + i, n), t).start()
+    own = pltpu.make_async_copy(m6, landing(s), load_sem.at[2])
+    own.start()
 
     for i in range(1, n):
         to = lax.rem(t + i, n)
@@ -391,25 +408,12 @@
         for u in range(nu):
             remote(m4.at[u], r4.at[u, s], s4.at[u, 0], e4.at[u, s], t, t).wait_send()
 
-    outs = []
-    for c in range(nch):
-        ccol = slice(c * cw, (c + 1) * cw)
-        for i in range(1, n):
-            src = lax.rem(s + i, n)
-            remote(m5.at[c], r5.at[c, src], s5.at[c, i], e5.at[c, src], src, t).wait_recv()
-        result = x_v[:, ccol].astype(F32)
-        for src in range(n):
-            result = result + r5[c, src].astype(F32)
-        x_v[:, ccol] = result.astype(BF16)
-        outs.append(
-            pltpu.make_async_copy(x_v.at[:, ccol], out_hbm.at[:, ccol], out_sem.at[c])
-        )
-        outs[c].start()
-    for c in range(nch):
-        for i in range(1, n):
-            to = lax.rem(s + i, n)
-            remote(m5.at[c], r5.at[c, s], s5.at[c, i], e5.at[c, s], to, t).wait_send()
-        outs[c].wait()
+    remote(m5, r5, s5.at[0], e5.at[0], partner, t).wait_send()
+    own.wait()
+    for i in order:
+        src = lax.rem(s + i, n)
+        remote(m6, landing(s), s6.at[i], e6.at[s], src, t).wait_send()
+        remote(m6, landing(src), s6.at[i], e6.at[src], src, t).wait_recv()
 
 
 def per_device(n, tokens, gain, w_query, w_kv, w_out, cache, lengths, perm):
@@ -423,12 +427,12 @@
     unit = min(heads_per, PER_KV)
     nu = heads_per // unit
     nq = max(1, qc // 1024)
-    nch = max(1, cols // 1024)
-    cw = cols // nch
+    half = cols // 2
+    assert n % 2 == 0
     assert steps == STEPS and steps * req_dev == 8 and req == n * req_dev
     cfg = dict(
         n=n, rows=rows, req=req, req_dev=req_dev, block=block, qc=qc, kc=kc,
-        nq=nq, nc=4, unit=unit, nu=nu, nch=nch, cw=cw,
+        nq=nq, nc=4, unit=unit, nu=nu, half=half,
     )
     widest = qc // nq // LANES + kc // LANES
     w1 = (widest + 2) // 2 * LANES
@@ -440,9 +444,9 @@
     smem = pl.BlockSpec(memory_space=pltpu.SMEM)
     vmem = pl.BlockSpec(memory_space=pltpu.VMEM)
     dma = pltpu.SemaphoreType.DMA
-    out = pl.pallas_call(
+    sums = pl.pallas_call(
         functools.partial(kernel, cfg),
-        out_shape=jax.ShapeDtypeStruct((rows, cols), BF16),
+        out_shape=jax.ShapeDtypeStruct((n // 2, rows, cols), BF16),
         in_specs=[smem, smem, vmem, vmem] + [any_spec] * 5,
         out_specs=any_spec,
         scratch_shapes=[
@@ -453,6 +457,7 @@
             pltpu.VMEM((block + LANES, cache.shape[2]), BF16),
             pltpu.VMEM((8, block + LANES), F32),
             pltpu.VMEM((rows, cols), F32),
+            pltpu.VMEM((2, rows, half), F32),
             pltpu.VMEM((nq, n, 16, w1), BF16),
             pltpu.VMEM((nq, n, 16, w1), BF16),
             pltpu.VMEM((nq, 16, w2), BF16),
@@ -463,17 +468,18 @@
             pltpu.VMEM((nu, n, 8, LANES), F32),
             pltpu.VMEM((nu, 16, w3), BF16),
             pltpu.VMEM((nu, n, 16, w3), BF16),
-            pltpu.VMEM((nch, rows, cw), BF16),
-            pltpu.VMEM((nch, n, rows, cw), BF16),
-            dma((2,)),
+            pltpu.VMEM((rows, half), BF16),
+            pltpu.VMEM((rows, half), BF16),
+            pltpu.VMEM((rows, half), BF16),
+            dma((3,)),
             dma((nq,)),
             dma((cfg["nc"],)),
             dma((nu,)),
-            dma((nch,)),
         ]
         + [dma((nq, n))] * 4
         + [dma((nu, n))] * 6
-        + [dma((nch, n))] * 2,
+        + [dma((1,))] * 2
+        + [dma((n,))] * 2,
         compiler_params=pltpu.CompilerParams(
             collective_id=0, has_side_effects=True, vmem_limit_bytes=56 * 1024 * 1024
         ),
@@ -486,7 +492,8 @@
         perm, lengths, gain, inv,
         tokens.reshape(rows, feat), w_query, w_kv, w_out, cache,
     )
-    return out.reshape(steps, req, cols)
+    summed = functools.reduce(jnp.add, [sums[c].astype(F32) for c in range(n // 2)])
+    return (tokens.astype(F32) + summed.reshape(steps, req, cols)).astype(BF16)
 
 
 def solution(mesh):

time: 42.1 us -> 39.9 us (0.948)
  Pallas kernels: 40.3 us -> 38.1 us
  other arithmetic: 0 us -> 1.69 us
  local copies, waits for them, and re-layouts: 1.57 us -> 0.01 us
    pallas_call x1, Pallas kernels: 40.3 us -> 38.1 us  [per_device(): pl.pallas_call(functools.partial(kernel, cfg), out_shape=jax.ShapeDtypeSt...]
    unnamed x1 -> x2, local copies, waits for them, and re-layouts: 1.57 us -> 0.01 us
    add x0 -> x1, other arithmetic: none -> 1 us  [per_device(): functools.reduce(jnp.add, [sums[c].astype(F32) for c in range(n // 2)])]
    convert_element_type x0 -> x1, other arithmetic: none -> 0.69 us  [per_device(): return (tokens.astype(F32) + summed.reshape(steps, req, cols)).astype(BF16)]
where the time goes in v3:
time: 39.9 us; the launch traced here: 39.8 us
  Pallas kernels  38.1 us (95%)
  other arithmetic  1.69 us (4%)
    pallas_call x1, Pallas kernels, per_device(): pl.pallas_call(functools.partial(kernel, cfg), out_shape=jax.ShapeDtypeSt...  38.1 us
    add x1, other arithmetic, per_device(): functools.reduce(jnp.add, [sums[c].astype(F32) for c in range(n // 2)])  1 us

profile of v3, /device:TPU:1, one launch (start us, length us, event | category | flops | bytes accessed | tf_op | source)
XLA Modules:
  0.0 39.8 jit_solution(17312999279901298093)
XLA Ops:
  0.0 0.0 copy-start
  0.0 38.1 %shard_map.91 = bf16[2,32,2048]{2,1,0:T(8,128)(2,1)} custom-call(s32[16]{0:T(128)} %perm_ref.1, s32[1,4]{1,0:T(1,128)} %len_ref.1, bf16[2048]{0:T(1024)(128)(2,1)} %gain_ref.1, f32[1,128]{1,0:T(1,128)} %constant.2.clone.inv_ref, bf16[32,2048]{1,0:T(8,128)(2,1)} %bitcast.3, bf16[2048,2048]{1,0:T(8,128)(2,1)} %wq_hbm.1, bf16[2048,512]{1,0:T(8,128)(2,1)} %wkv_hbm.1, ...), custom_call_target="tpu_custom_call" | custom-call | flops 1409286144 | bytes 31457280 | tf_op jit(solution)/shard_map/pallas_call | solution.py:447
  38.1 1.0 %convert_add_fusion = f32[1,32,2048]{2,1,0:T(8,128)S(1)} fusion(bf16[2,32,2048]{2,1,0:T(8,128)(2,1)} %shard_map.91), kind=kLoop, calls=%fused_computation.1 | loop fusion | flops 196608 | bytes 524288 | tf_op jit(solution)/shard_map/add | solution.py:495
  39.1 0.0 copy-done
  39.1 0.7 %add_convert_fusion = bf16[2,16,2048]{2,1,0:T(8,128)(2,1)} fusion(f32[2,16,2048]{2,1,0:T(8,128)S(1)} %bitcast.2, bf16[2,16,2048]{2,1,0:T(8,128)(2,1)S(1)} %copy-done), kind=kLoop, calls=%fused_computation | loop fusion | flops 196608 | bytes 524288 | tf_op jit(solution)/shard_map/convert_element_type | solution.py:496
Async XLA Ops:
  0.0 39.1 %copy-start = (bf16[2,16,2048]{2,1,0:T(8,128)(2,1)S(1)}, bf16[2,16,2048]{2,1,0:T(8,128)(2,1)}, u32[]{:S(2)}) copy-start(bf16[2,16,2048]{2,1,0:T(8,128)(2,1)} %param.9) | copy-start | bytes 393220

commit v4 on v3

--- a/solution.py
+++ b/solution.py
@@ -44,7 +44,7 @@
     cfg,
     perm_ref, len_ref, gain_ref, inv_ref, x_hbm, wq_hbm, wkv_hbm, wo_hbm, cache_hbm,
     out_hbm,
-    x_v, wq_v, wkv_v, wo_v, kv_v, bias_v, fin_v, part_v,
+    x_v, wq_v, wkv_v, wo_v, kv_v, bias_v, fin_v,
     m1, r1, m2, r2, m3, r3, st, rst, m4, r4, m5, r5, m6,
     load_sem, wq_sem, cache_sem, wo_sem,
     s1, e1, s2, e2, s3, e3, s3b, e3b, s4, e4, s5, e5, s6, e6,
@@ -359,20 +359,16 @@
     core = lax.rem(s, 2)
     partner = s + 1 - 2 * core
     u = nu - 1
-    for c in range(2):
-        ccol = slice(c * half, (c + 1) * half)
+    def half_sum(c):
+        ccol = pl.ds(pl.multiple_of(c * half, half), half)
         part = jnp.dot(lefts[u], wo_v[u * uw : (u + 1) * uw, ccol], preferred_element_type=F32)
-        if nu > 1:
-            part = part + fin_v[:, ccol]
-        part_v[c] = part
-
-        @pl.when(core != c)
-        def _():
-            m5[...] = part.astype(BF16)
-            remote(m5, r5, s5.at[0], e5.at[0], partner, t).start()
-
+        return part + fin_v[:, ccol] if nu > 1 else part
+
+    m5[...] = half_sum(1 - core).astype(BF16)
+    remote(m5, r5, s5.at[0], e5.at[0], partner, t).start()
+    kept = half_sum(core)
     remote(m5, r5, s5.at[0], e5.at[0], partner, t).wait_recv()
-    m6[...] = (part_v[core] + r5[...].astype(F32)).astype(BF16)
+    m6[...] = (kept + r5[...].astype(F32)).astype(BF16)
 
     def landing(src):
         return out_hbm.at[
@@ -457,7 +453,6 @@
             pltpu.VMEM((block + LANES, cache.shape[2]), BF16),
             pltpu.VMEM((8, block + LANES), F32),
             pltpu.VMEM((rows, cols), F32),
-            pltpu.VMEM((2, rows, half), F32),
             pltpu.VMEM((nq, n, 16, w1), BF16),
             pltpu.VMEM((nq, n, 16, w1), BF16),
             pltpu.VMEM((nq, 16, w2), BF16),

time: 39.9 us -> 39.9 us (level)
  no operation moved by 1% of the time
where the time goes in v4:
time: 39.9 us; the launch traced here: 39.7 us
  Pallas kernels  38 us (95%)
  other arithmetic  1.69 us (4%)
    pallas_call x1, Pallas kernels, per_device(): pl.pallas_call(functools.partial(kernel, cfg), out_shape=jax.ShapeDtypeSt...  38 us
    add x1, other arithmetic, per_device(): functools.reduce(jnp.add, [sums[c].astype(F32) for c in range(n // 2)])  1 us

profile of v4, /device:TPU:1, one launch (start us, length us, event | category | flops | bytes accessed | tf_op | source)
XLA Modules:
  0.0 39.7 jit_solution(9039821928909771714)
XLA Ops:
  0.0 0.0 copy-start
  0.0 38.0 %shard_map.91 = bf16[2,32,2048]{2,1,0:T(8,128)(2,1)} custom-call(s32[16]{0:T(128)} %perm_ref.1, s32[1,4]{1,0:T(1,128)} %len_ref.1, bf16[2048]{0:T(1024)(128)(2,1)} %gain_ref.1, f32[1,128]{1,0:T(1,128)} %constant.2.clone.inv_ref, bf16[32,2048]{1,0:T(8,128)(2,1)} %bitcast.3, bf16[2048,2048]{1,0:T(8,128)(2,1)} %wq_hbm.1, bf16[2048,512]{1,0:T(8,128)(2,1)} %wkv_hbm.1, ...), custom_call_target="tpu_custom_call" | custom-call | flops 1409286144 | bytes 31457280 | tf_op jit(solution)/shard_map/pallas_call | solution.py:443
  38.0 1.0 %convert_add_fusion = f32[1,32,2048]{2,1,0:T(8,128)S(1)} fusion(bf16[2,32,2048]{2,1,0:T(8,128)(2,1)} %shard_map.91), kind=kLoop, calls=%fused_computation.1 | loop fusion | flops 196608 | bytes 524288 | tf_op jit(solution)/shard_map/add | solution.py:490
  39.0 0.0 copy-done
  39.0 0.7 %add_convert_fusion = bf16[2,16,2048]{2,1,0:T(8,128)(2,1)} fusion(f32[2,16,2048]{2,1,0:T(8,128)S(1)} %bitcast.2, bf16[2,16,2048]{2,1,0:T(8,128)(2,1)S(1)} %copy-done), kind=kLoop, calls=%fused_computation | loop fusion | flops 196608 | bytes 524288 | tf_op jit(solution)/shard_map/convert_element_type | solution.py:491
Async XLA Ops:
  0.0 39.0 %copy-start = (bf16[2,16,2048]{2,1,0:T(8,128)(2,1)S(1)}, bf16[2,16,2048]{2,1,0:T(8,128)(2,1)}, u32[]{:S(2)}) copy-start(bf16[2,16,2048]{2,1,0:T(8,128)(2,1)} %param.9) | copy-start | bytes 393220
